TPU v7x, 256 devices: a whole 4x4x8 slice. The times are simulated.
256 devices in a mesh: grp: 16 (over x, y), tp: 16 (over z, core).
Axes of the slice: x: 4, y: 4, z: 8, core: 2. Of those that a mesh axis runs over, the one named last changes fastest.
Arguments:
- tokens: bfloat16 [12288, 3584], P(('grp', 'tp')), parts along dimension 0, may hold values from -6 to 6
- counts: int32 [256], P(('grp', 'tp')), parts along dimension 0, may hold values from 16 to 48, as said below
- norm_gain: float32 [3584], replicated, may hold values from 0.1 to 1.9
- gate_weight: bfloat16 [3584, 9216], P(None, 'tp'), may hold values from -0.09375 to 0.09375
- up_weight: bfloat16 [3584, 9216], P(None, 'tp'), may hold values from -0.09375 to 0.09375
- down_weight: bfloat16 [9216, 3584], P('tp'), may hold values from -0.0625 to 0.0625
Outputs:
- mixed: bfloat16 [12288, 3584], P(('grp', 'tp')), parts along dimension 0
There are 16 independent parts, one for each index of `grp`. A program takes and returns all parts, laid end to end along the dimension named above; an argument that names none is the same for every part. Nothing has to cross between parts.
Inputs may be any that keep to these rules, and one draw needn't show every extreme that they name: `counts`: each device holds from 16 to 48 live requests in its first slots; in every group some device holds exactly 48 and another exactly 16.
All inputs are finite; a program needn't handle non-finite values.
Results may differ from a plain program's by a relative error of at most 0.023.
Values may be sent and summed in bfloat16 or wider, within the bound.
No kernel may reach another device: no remote copies, remote signals or barrier semaphores. Data moves between devices by JAX's collectives and lax.ppermute only.
A program may use at most 64 MiB of HBM per device.

v0:
```python
import jax
import jax.numpy as jnp
from jax import lax
from jax.experimental import pallas as pl
from jax.experimental.pallas import tpu as pltpu
from jax.sharding import PartitionSpec as P

CHUNKS = 3
HOP_BYTES = 9_000_000
IN_VMEM = pl.BlockSpec(memory_space=pltpu.VMEM)


def local(kernel, shape, operands, specs=None, bytes_accessed=HOP_BYTES):
    return pl.pallas_call(
        kernel,
        out_shape=jax.ShapeDtypeStruct(shape, jnp.bfloat16),
        in_specs=specs or [IN_VMEM] * len(operands),
        out_specs=IN_VMEM,
        compiler_params=pltpu.CompilerParams(vmem_limit_bytes=3 << 20),
        cost_estimate=pl.CostEstimate(flops=0, bytes_accessed=bytes_accessed, transcendentals=0),
    )(*operands)


def by_columns(width, step, work):
    def one(index, none):
        work(pl.ds(pl.multiple_of(index * step, step), step))
        return none

    lax.fori_loop(0, width // step, one, 0)


def normalize(tokens, gain):
    slots, width = tokens.shape

    def kernel(tokens_ref, gain_ref, normed_ref):
        def one(index, none):
            rows = pl.ds(pl.multiple_of(index * 16, 16), 16)
            widened = tokens_ref[rows, :].astype(jnp.float32)
            scale_row = lax.rsqrt(jnp.sum(widened * widened, axis=-1, keepdims=True) / width + 1e-06)
            normed_ref[rows, :] = (widened * scale_row * gain_ref[...].reshape(1, width)).astype(normed_ref.dtype)
            return none

        lax.fori_loop(0, slots // 16, one, 0)

    return local(kernel, tokens.shape, (tokens, gain))


def pack(*blocks):
    rows = [block.shape[0] for block in blocks]

    def kernel(*refs):
        def work(columns):
            at = 0
            for ref, count in zip(refs, rows):
                refs[-1][pl.ds(at, count), columns] = ref[:, columns]
                at += count

        by_columns(blocks[0].shape[1], 512, work)

    return local(kernel, (sum(rows), blocks[0].shape[1]), blocks)


def join(size, *terms):
    spans = [(at, rows) for _, at, rows in terms]

    def kernel(*refs):
        cut = min(rows for _, rows in spans)

        def work(columns):
            for low, high in ((0, cut), (cut, size)):
                if low < high:
                    total = None
                    for ref, (at, rows) in zip(refs, spans):
                        if rows >= high:
                            value = ref[pl.ds(at + low, high - low), columns].astype(jnp.float32)
                            total = value if total is None else total + value
                    refs[-1][pl.ds(low, high - low), columns] = total.astype(refs[-1].dtype)

        by_columns(terms[0][0].shape[1], 512, work)

    return local(kernel, (size, terms[0][0].shape[1]), [array for array, _, _ in terms])


def body(tokens, counts, norm_gain, gate_weight, up_weight, down_weight):
    slots, width = tokens.shape
    members = lax.axis_size("tp")
    chips = members // 2
    part = slots // CHUNKS
    both = 2 * part

    swap_pairs = [(i, i ^ 1) for i in range(members)]
    ring_pairs = [(2 * z, 2 * ((z + 1) % chips)) for z in range(chips)]
    ring_pairs += [(2 * z + 1, 2 * ((z - 1) % chips) + 1) for z in range(chips)]

    def swap(value):
        return lax.ppermute(value, "tp", swap_pairs)

    def ring(value):
        return lax.ppermute(value, "tp", ring_pairs)

    f32 = jnp.float32
    bf16 = jnp.bfloat16
    token = counts

    def order(*values):
        nonlocal token
        token, *values = lax.optimization_barrier((token, *values))
        return values if len(values) > 1 else values[0]

    def concat(*values):
        return order(pack(*order(*values)))

    batch = {}
    gate_rows, up_rows, down_rows = gate_weight.T, up_weight.T, down_weight

    def gate_of(name):
        rows, weight = order(batch[name], gate_rows)
        batch[name] = rows, order(lax.dot_general(rows, weight, (((1,), (1,)), ((), ())), preferred_element_type=f32))

    def hidden_of(name):
        rows, gate, weight = order(*batch[name], up_rows)
        up_part = lax.dot_general(rows, weight, (((1,), (1,)), ((), ())), preferred_element_type=f32)
        batch[name] = order((jax.nn.silu(gate) * up_part).astype(bf16))

    def partial_of(name):
        hidden, weight = order(batch[name], down_rows)
        batch[name] = order(jnp.dot(hidden, weight, preferred_element_type=f32).astype(bf16))

    chunks = range(CHUNKS)
    normed = order(normalize(*order(tokens, norm_gain)))
    swapped = order(swap(normed))
    own, flight = [], []
    for i in chunks:
        rows = slice(i * part, (i + 1) * part)
        own.append(concat(normed[rows], swapped[rows]))
        flight.append(ring(own[i]))

    mine = {}
    other = {}

    def arrive(hop, i):
        block = order(flight[i])
        mine[hop, i] = block
        if hop < 3:
            flight[i] = ring(block)
        elif hop == 3:
            flight[i] = ring(block[:part])

    waiting = []

    def receive(hop, i):
        arrive(hop, i)
        if len(waiting) == 2:
            key = waiting.pop(0)
            other[key] = order(other[key])
        other[hop, i] = swap(mine[hop, i])
        waiting.append((hop, i))

    receive(1, 0)
    receive(1, 1)
    receive(1, 2)
    receive(2, 0)
    batch["a"] = concat(*own, *[mine[1, i] for i in chunks], other[1, 0], other[1, 1])
    gate_of("a")
    receive(2, 1)
    hidden_of("a")
    receive(2, 2)
    partial_of("a")
    receive(3, 0)
    receive(3, 1)
    batch["b"] = concat(other[1, 2], *[other[2, i] for i in chunks], *[mine[2, i] for i in chunks], mine[3, 0])
    gate_of("b")
    receive(3, 2)
    hidden_of("b")
    arrive(4, 0)
    key = waiting.pop(0)
    other[key] = order(other[key])
    partial_of("b")
    arrive(4, 1)
    moved_2 = swap(batch["b"][4 * both:])
    arrive(4, 2)
    key = waiting.pop(0)
    other[key] = order(other[key])
    fourth = concat(*[mine[4, i] for i in chunks])
    fifth = order(swap(fourth))
    last = [other[3, i] for i in chunks] + [mine[3, 1], mine[3, 2]]
    batch["c"] = concat(*last, fourth, fifth)
    gate_of("c")
    hidden_of("c")
    partial_of("c")
    moved_4 = order(swap(batch["c"][3 * both:5 * both + 3 * part]))
    moved_1 = None

    def depart(hop, i):
        size = part if hop == 4 else both
        terms = []
        if hop == 4:
            terms = [(batch["c"], 5 * both + 3 * part + i * part, part), (moved_4, 2 * both + i * part, part)]
        elif hop == 3:
            there = (moved_2, 3 * both, both) if i == 0 else (moved_4, (i - 1) * both, both)
            terms = [(batch["c"], i * both, both), there, (flight[i], 0, part)]
        elif hop == 2:
            terms = [(batch["b"], (1 + i) * both, both), (moved_2, i * both, both), (flight[i], 0, both)]
        elif hop == 1:
            here = (batch["b"], 0, both) if i == 2 else (batch["a"], (6 + i) * both, both)
            terms = [here, (moved_1, i * both, both), (flight[i], 0, both)]
        arrays = order(*[array for array, _, _ in terms])
        terms = [(array, at, rows) for array, (_, at, rows) in zip(arrays, terms)]
        flight[i] = ring(order(join(size, *terms)))

    for i in chunks:
        depart(4, i)
    moved_1 = swap(batch["a"][3 * both:6 * both])
    for hop in (3, 2, 1):
        for i in chunks:
            depart(hop, i)
    given = []
    for i in chunks:
        carry, mixed = order(flight[i], batch["a"])
        flight[i] = carry
        given.append(swap(order(join(part, (mixed, i * both + part, part), (carry, 0, part)))))
    done = []
    for i in chunks:
        carry, mixed, gift = order(flight[i], batch["a"], given[i])
        done.append(carry[part:].astype(f32) + mixed[i * both:i * both + part].astype(f32) + gift.astype(f32))
    alive = jnp.arange(slots, dtype=jnp.int32) < token[0]
    return jnp.where(alive[:, None], jnp.concatenate(done, 0), 0.0).astype(bf16)


def solution(mesh):
    in_specs = (
        P(("grp", "tp"), None),
        P(("grp", "tp")),
        P(),
        P(None, "tp"),
        P(None, "tp"),
        P("tp", None),
    )
    out_specs = P(("grp", "tp"), None)
    return jax.shard_map(body, mesh=mesh, in_specs=in_specs, out_specs=out_specs, check_vma=False)
```

profile of v0, /device:TPU:1, one launch (start us, length us, event | category | flops | bytes accessed | tf_op | source)
XLA Modules:
  0.0 91.8 jit_solution(8699248743063739616)
XLA Ops:
  2.1 3.3 %collective-permute-start = (bf16[48,3584]{1,0:T(8,128)(2,1)S(1)}, bf16[48,3584]{1,0:T(8,128)(2,1)S(1)}, u32[]{:S(2)}, u32[]{:S(2)}) collective-permute-start(bf16[48,3584]{1,0:T(8,128)(2,1)S(1)} %shard_map.64), channel_id=1, source_target_pairs={{0,1},{1,0},{2,3},{3,2},{4,5},{5,4},{6,7},{7,6},{8,9},{9,8},{10,11... | collective-permute-start | bytes 1032200 | tf_op jit(solution)/shard_map/ppermute | solution.py:96
  6.8 3.9 %collective-permute-start.1 = (bf16[32,3584]{1,0:T(8,128)(2,1)S(1)}, bf16[32,3584]{1,0:T(8,128)(2,1)S(1)}, u32[]{:S(2)}, u32[]{:S(2)}) collective-permute-start(bf16[32,3584]{1,0:T(8,128)(2,1)S(1)} %shard_map.65.refs_0_), channel_id=1, source_target_pairs={{0,2},{2,4},{4,6},{6,8},{8,10},{10,12},{12,14},{14,0},{1,15},{3,1}... | collective-permute-start | bytes 688136 | tf_op jit(solution)/shard_map/ppermute | solution.py:99
  12.4 1.3 %collective-permute-done.1.refs_3_ = bf16[32,3584]{1,0:T(8,128)(2,1)S(1)} collective-permute-done((bf16[32,3584]{1,0:T(8,128)(2,1)S(1)}, bf16[32,3584]{1,0:T(8,128)(2,1)S(1)}, u32[]{:S(2)}, u32[]{:S(2)}) %collective-permute-start.1) | collective-permute-done | bytes 229408 | tf_op jit(solution)/shard_map/ppermute | solution.py:99
  13.7 1.7 %collective-permute-start.4 = (bf16[32,3584]{1,0:T(8,128)(2,1)S(1)}, bf16[32,3584]{1,0:T(8,128)(2,1)S(1)}, u32[]{:S(2)}, u32[]{:S(2)}) collective-permute-start(bf16[32,3584]{1,0:T(8,128)(2,1)S(1)} %collective-permute-done.1.refs_3_), channel_id=1, source_target_pairs={{0,1},{1,0},{2,3},{3,2},{4,5},{5,4},{6,7},{7,6},{8,9},{9,8},{10,11... | collective-permute-start | bytes 688136 | tf_op jit(solution)/shard_map/ppermute | solution.py:96
  15.4 1.7 %collective-permute-start.5 = (bf16[32,3584]{1,0:T(8,128)(2,1)S(1)}, bf16[32,3584]{1,0:T(8,128)(2,1)S(1)}, u32[]{:S(2)}, u32[]{:S(2)}) collective-permute-start(bf16[32,3584]{1,0:T(8,128)(2,1)S(1)} %collective-permute-done.1.refs_3_), channel_id=1, source_target_pairs={{0,2},{2,4},{4,6},{6,8},{8,10},{10,12},{12,14},{14,0},{1,15},{3,1}... | collective-permute-start | bytes 688136 | tf_op jit(solution)/shard_map/ppermute | solution.py:99
  17.8 1.7 %collective-permute-start.7 = (bf16[32,3584]{1,0:T(8,128)(2,1)S(1)}, bf16[32,3584]{1,0:T(8,128)(2,1)S(1)}, u32[]{:S(2)}, u32[]{:S(2)}) collective-permute-start(bf16[32,3584]{1,0:T(8,128)(2,1)S(1)} %collective-permute-done.2.refs_4_), channel_id=1, source_target_pairs={{0,2},{2,4},{4,6},{6,8},{8,10},{10,12},{12,14},{14,0},{1,15},{3,1}... | collective-permute-start | bytes 688136 | tf_op jit(solution)/shard_map/ppermute | solution.py:99
  20.3 1.7 %collective-permute-start.9 = (bf16[32,3584]{1,0:T(8,128)(2,1)S(1)}, bf16[32,3584]{1,0:T(8,128)(2,1)S(1)}, u32[]{:S(2)}, u32[]{:S(2)}) collective-permute-start(bf16[32,3584]{1,0:T(8,128)(2,1)S(1)} %collective-permute-done.3.refs_5_), channel_id=1, source_target_pairs={{0,2},{2,4},{4,6},{6,8},{8,10},{10,12},{12,14},{14,0},{1,15},{3,1}... | collective-permute-start | bytes 688136 | tf_op jit(solution)/shard_map/ppermute | solution.py:99
  22.8 1.7 %collective-permute-start.11 = (bf16[32,3584]{1,0:T(8,128)(2,1)S(1)}, bf16[32,3584]{1,0:T(8,128)(2,1)S(1)}, u32[]{:S(2)}, u32[]{:S(2)}) collective-permute-start(bf16[32,3584]{1,0:T(8,128)(2,1)S(1)} %collective-permute-done.5.refs_4_), channel_id=1, source_target_pairs={{0,2},{2,4},{4,6},{6,8},{8,10},{10,12},{12,14},{14,0},{1,15},{3,1}... | collective-permute-start | bytes 688136 | tf_op jit(solution)/shard_map/ppermute | solution.py:99
  28.6 2.2 %collective-permute-start.15 = (bf16[32,3584]{1,0:T(8,128)(2,1)S(1)}, bf16[32,3584]{1,0:T(8,128)(2,1)S(1)}, u32[]{:S(2)}, u32[]{:S(2)}) collective-permute-start(bf16[32,3584]{1,0:T(8,128)(2,1)S(1)} %collective-permute-done.9.refs_6_), channel_id=1, source_target_pairs={{0,2},{2,4},{4,6},{6,8},{8,10},{10,12},{12,14},{14,0},{1,15},{3,1}... | collective-permute-start | bytes 688136 | tf_op jit(solution)/shard_map/ppermute | solution.py:99
  30.9 1.6 %convolution_convert_fusion.2.refs_0_ = bf16[256,3584]{1,0:T(8,128)(2,1)S(1)} fusion(bf16[256,576]{0,1:T(8,128)(2,1)S(1)} %fusion, bf16[576,3584]{1,0:T(8,128)(2,1)S(1)} %copy-done.2), kind=kOutput, calls=%fused_computation.2 | convolution fusion | flops 1057882112 | bytes 6258688 | tf_op jit(solution)/shard_map/dot_general | solution.py:127
  40.1 1.6 %convolution_convert_fusion.1.refs_0_ = bf16[256,3584]{1,0:T(8,128)(2,1)S(1)} fusion(bf16[256,576]{0,1:T(8,128)(2,1)S(1)} %fusion.1, bf16[576,3584]{1,0:T(8,128)(2,1)S(1)} %copy-done.2), kind=kOutput, calls=%fused_computation.1 | convolution fusion | flops 1057882112 | bytes 6258688 | tf_op jit(solution)/shard_map/dot_general | solution.py:127
  42.9 2.2 %collective-permute-start.22 = (bf16[48,3584]{1,0:T(8,128)(2,1)S(1)}, bf16[48,3584]{1,0:T(8,128)(2,1)S(1)}, u32[]{:S(2)}, u32[]{:S(2)}) collective-permute-start(bf16[48,3584]{1,0:T(8,128)(2,1)S(1)} %shard_map.70.refs_5_), channel_id=1, source_target_pairs={{0,1},{1,0},{2,3},{3,2},{4,5},{5,4},{6,7},{7,6},{8,9},{9,8},{10,11... | collective-permute-start | bytes 1032200 | tf_op jit(solution)/shard_map/ppermute | solution.py:96
  45.1 1.3 %collective-permute-done.22.refs_6_ = bf16[48,3584]{1,0:T(8,128)(2,1)S(1)} collective-permute-done((bf16[48,3584]{1,0:T(8,128)(2,1)S(1)}, bf16[48,3584]{1,0:T(8,128)(2,1)S(1)}, u32[]{:S(2)}, u32[]{:S(2)}) %collective-permute-start.22) | collective-permute-done | bytes 344096 | tf_op jit(solution)/shard_map/ppermute | solution.py:96
  49.1 1.6 %convolution_convert_fusion.refs_0_ = bf16[256,3584]{1,0:T(8,128)(2,1)S(1)} fusion(bf16[256,576]{0,1:T(8,128)(2,1)S(1)} %fusion.2, bf16[576,3584]{1,0:T(8,128)(2,1)S(1)} %copy-done.2), kind=kOutput, calls=%fused_computation | convolution fusion | flops 1057882112 | bytes 6258688 | tf_op jit(solution)/shard_map/dot_general | solution.py:127
  57.1 1.8 %collective-permute-start.28 = (bf16[32,3584]{1,0:T(8,128)(2,1)S(1)}, bf16[32,3584]{1,0:T(8,128)(2,1)S(1)}, u32[]{:S(2)}, u32[]{:S(2)}) collective-permute-start(bf16[32,3584]{1,0:T(8,128)(2,1)S(1)} %shard_map.75), channel_id=1, source_target_pairs={{0,2},{2,4},{4,6},{6,8},{8,10},{10,12},{12,14},{14,0},{1,15},{3,1}... | collective-permute-start | bytes 688136 | tf_op jit(solution)/shard_map/ppermute | solution.py:99
  62.3 2.9 %collective-permute-start.32 = (bf16[32,3584]{1,0:T(8,128)(2,1)S(1)}, bf16[32,3584]{1,0:T(8,128)(2,1)S(1)}, u32[]{:S(2)}, u32[]{:S(2)}) collective-permute-start(bf16[32,3584]{1,0:T(8,128)(2,1)S(1)} %shard_map.78), channel_id=1, source_target_pairs={{0,2},{2,4},{4,6},{6,8},{8,10},{10,12},{12,14},{14,0},{1,15},{3,1}... | collective-permute-start | bytes 688136 | tf_op jit(solution)/shard_map/ppermute | solution.py:99
  65.3 2.3 %collective-permute-start.33 = (bf16[32,3584]{1,0:T(8,128)(2,1)S(1)}, bf16[32,3584]{1,0:T(8,128)(2,1)S(1)}, u32[]{:S(2)}, u32[]{:S(2)}) collective-permute-start(bf16[32,3584]{1,0:T(8,128)(2,1)S(1)} %shard_map.79), channel_id=1, source_target_pairs={{0,2},{2,4},{4,6},{6,8},{8,10},{10,12},{12,14},{14,0},{1,15},{3,1}... | collective-permute-start | bytes 688136 | tf_op jit(solution)/shard_map/ppermute | solution.py:99
  67.8 2.3 %collective-permute-start.34 = (bf16[32,3584]{1,0:T(8,128)(2,1)S(1)}, bf16[32,3584]{1,0:T(8,128)(2,1)S(1)}, u32[]{:S(2)}, u32[]{:S(2)}) collective-permute-start(bf16[32,3584]{1,0:T(8,128)(2,1)S(1)} %shard_map.80), channel_id=1, source_target_pairs={{0,2},{2,4},{4,6},{6,8},{8,10},{10,12},{12,14},{14,0},{1,15},{3,1}... | collective-permute-start | bytes 688136 | tf_op jit(solution)/shard_map/ppermute | solution.py:99
  70.3 1.9 %collective-permute-done.33.refs_2_ = bf16[32,3584]{1,0:T(8,128)(2,1)S(1)} collective-permute-done((bf16[32,3584]{1,0:T(8,128)(2,1)S(1)}, bf16[32,3584]{1,0:T(8,128)(2,1)S(1)}, u32[]{:S(2)}, u32[]{:S(2)}) %collective-permute-start.33) | collective-permute-done | bytes 229408 | tf_op jit(solution)/shard_map/ppermute | solution.py:99
  72.2 2.7 %collective-permute-start.35 = (bf16[32,3584]{1,0:T(8,128)(2,1)S(1)}, bf16[32,3584]{1,0:T(8,128)(2,1)S(1)}, u32[]{:S(2)}, u32[]{:S(2)}) collective-permute-start(bf16[32,3584]{1,0:T(8,128)(2,1)S(1)} %shard_map.81), channel_id=1, source_target_pairs={{0,2},{2,4},{4,6},{6,8},{8,10},{10,12},{12,14},{14,0},{1,15},{3,1}... | collective-permute-start | bytes 688136 | tf_op jit(solution)/shard_map/ppermute | solution.py:99
  75.3 2.2 %collective-permute-start.37 = (bf16[32,3584]{1,0:T(8,128)(2,1)S(1)}, bf16[32,3584]{1,0:T(8,128)(2,1)S(1)}, u32[]{:S(2)}, u32[]{:S(2)}) collective-permute-start(bf16[32,3584]{1,0:T(8,128)(2,1)S(1)} %shard_map.83), channel_id=1, source_target_pairs={{0,2},{2,4},{4,6},{6,8},{8,10},{10,12},{12,14},{14,0},{1,15},{3,1}... | collective-permute-start | bytes 688136 | tf_op jit(solution)/shard_map/ppermute | solution.py:99
  77.9 2.4 %collective-permute-done.36.refs_1_ = bf16[32,3584]{1,0:T(8,128)(2,1)S(1)} collective-permute-done((bf16[32,3584]{1,0:T(8,128)(2,1)S(1)}, bf16[32,3584]{1,0:T(8,128)(2,1)S(1)}, u32[]{:S(2)}, u32[]{:S(2)}) %collective-permute-start.36) | collective-permute-done | bytes 229408 | tf_op jit(solution)/shard_map/ppermute | solution.py:99
  80.3 2.4 %collective-permute-done.37.refs_1_ = bf16[32,3584]{1,0:T(8,128)(2,1)S(1)} collective-permute-done((bf16[32,3584]{1,0:T(8,128)(2,1)S(1)}, bf16[32,3584]{1,0:T(8,128)(2,1)S(1)}, u32[]{:S(2)}, u32[]{:S(2)}) %collective-permute-start.37) | collective-permute-done | bytes 229408 | tf_op jit(solution)/shard_map/ppermute | solution.py:99
  82.7 6.4 %collective-permute-start.38 = (bf16[16,3584]{1,0:T(8,128)(2,1)S(1)}, bf16[16,3584]{1,0:T(8,128)(2,1)S(1)}, u32[]{:S(2)}, u32[]{:S(2)}) collective-permute-start(bf16[16,3584]{1,0:T(8,128)(2,1)S(1)} %shard_map.84), channel_id=1, source_target_pairs={{0,1},{1,0},{2,3},{3,2},{4,5},{5,4},{6,7},{7,6},{8,9},{9,8},{10,11... | collective-permute-start | bytes 344072 | tf_op jit(solution)/shard_map/ppermute | solution.py:96
  (112 shorter events, 35.5 us)
Async XLA Ops:
  6.8 6.9 %collective-permute-start.1 = (bf16[32,3584]{1,0:T(8,128)(2,1)S(1)}, bf16[32,3584]{1,0:T(8,128)(2,1)S(1)}, u32[]{:S(2)}, u32[]{:S(2)}) collective-permute-start(bf16[32,3584]{1,0:T(8,128)(2,1)S(1)} %shard_map.65.refs_0_), channel_id=1, source_target_pairs={{0,2},{2,4},{4,6},{6,8},{8,10},{10,12},{12,14},{14,0},{1,15},{3,1}... | collective-permute-start | bytes 688136 | tf_op jit(solution)/shard_map/ppermute | solution.py:99
  10.8 6.4 %collective-permute-start.2 = (bf16[32,3584]{1,0:T(8,128)(2,1)S(1)}, bf16[32,3584]{1,0:T(8,128)(2,1)S(1)}, u32[]{:S(2)}, u32[]{:S(2)}) collective-permute-start(bf16[32,3584]{1,0:T(8,128)(2,1)S(1)} %shard_map.66.refs_1_), channel_id=1, source_target_pairs={{0,2},{2,4},{4,6},{6,8},{8,10},{10,12},{12,14},{14,0},{1,15},{3,1}... | collective-permute-start | bytes 688136 | tf_op jit(solution)/shard_map/ppermute | solution.py:99
  11.6 8.0 %collective-permute-start.3 = (bf16[32,3584]{1,0:T(8,128)(2,1)S(1)}, bf16[32,3584]{1,0:T(8,128)(2,1)S(1)}, u32[]{:S(2)}, u32[]{:S(2)}) collective-permute-start(bf16[32,3584]{1,0:T(8,128)(2,1)S(1)} %shard_map.67.refs_2_), channel_id=1, source_target_pairs={{0,2},{2,4},{4,6},{6,8},{8,10},{10,12},{12,14},{14,0},{1,15},{3,1}... | collective-permute-start | bytes 688136 | tf_op jit(solution)/shard_map/ppermute | solution.py:99
  13.7 6.6 %collective-permute-start.4 = (bf16[32,3584]{1,0:T(8,128)(2,1)S(1)}, bf16[32,3584]{1,0:T(8,128)(2,1)S(1)}, u32[]{:S(2)}, u32[]{:S(2)}) collective-permute-start(bf16[32,3584]{1,0:T(8,128)(2,1)S(1)} %collective-permute-done.1.refs_3_), channel_id=1, source_target_pairs={{0,1},{1,0},{2,3},{3,2},{4,5},{5,4},{6,7},{7,6},{8,9},{9,8},{10,11... | collective-permute-start | bytes 688136 | tf_op jit(solution)/shard_map/ppermute | solution.py:96
  15.4 6.7 %collective-permute-start.5 = (bf16[32,3584]{1,0:T(8,128)(2,1)S(1)}, bf16[32,3584]{1,0:T(8,128)(2,1)S(1)}, u32[]{:S(2)}, u32[]{:S(2)}) collective-permute-start(bf16[32,3584]{1,0:T(8,128)(2,1)S(1)} %collective-permute-done.1.refs_3_), channel_id=1, source_target_pairs={{0,2},{2,4},{4,6},{6,8},{8,10},{10,12},{12,14},{14,0},{1,15},{3,1}... | collective-permute-start | bytes 688136 | tf_op jit(solution)/shard_map/ppermute | solution.py:99
  17.8 8.1 %collective-permute-start.7 = (bf16[32,3584]{1,0:T(8,128)(2,1)S(1)}, bf16[32,3584]{1,0:T(8,128)(2,1)S(1)}, u32[]{:S(2)}, u32[]{:S(2)}) collective-permute-start(bf16[32,3584]{1,0:T(8,128)(2,1)S(1)} %collective-permute-done.2.refs_4_), channel_id=1, source_target_pairs={{0,2},{2,4},{4,6},{6,8},{8,10},{10,12},{12,14},{14,0},{1,15},{3,1}... | collective-permute-start | bytes 688136 | tf_op jit(solution)/shard_map/ppermute | solution.py:99
  19.6 6.5 %collective-permute-start.8 = (bf16[32,3584]{1,0:T(8,128)(2,1)S(1)}, bf16[32,3584]{1,0:T(8,128)(2,1)S(1)}, u32[]{:S(2)}, u32[]{:S(2)}) collective-permute-start(bf16[32,3584]{1,0:T(8,128)(2,1)S(1)} %collective-permute-done.3.refs_5_), channel_id=1, source_target_pairs={{0,1},{1,0},{2,3},{3,2},{4,5},{5,4},{6,7},{7,6},{8,9},{9,8},{10,11... | collective-permute-start | bytes 688136 | tf_op jit(solution)/shard_map/ppermute | solution.py:96
  20.3 8.2 %collective-permute-start.9 = (bf16[32,3584]{1,0:T(8,128)(2,1)S(1)}, bf16[32,3584]{1,0:T(8,128)(2,1)S(1)}, u32[]{:S(2)}, u32[]{:S(2)}) collective-permute-start(bf16[32,3584]{1,0:T(8,128)(2,1)S(1)} %collective-permute-done.3.refs_5_), channel_id=1, source_target_pairs={{0,2},{2,4},{4,6},{6,8},{8,10},{10,12},{12,14},{14,0},{1,15},{3,1}... | collective-permute-start | bytes 688136 | tf_op jit(solution)/shard_map/ppermute | solution.py:99
  22.0 6.6 %collective-permute-start.10 = (bf16[32,3584]{1,0:T(8,128)(2,1)S(1)}, bf16[32,3584]{1,0:T(8,128)(2,1)S(1)}, u32[]{:S(2)}, u32[]{:S(2)}) collective-permute-start(bf16[32,3584]{1,0:T(8,128)(2,1)S(1)} %collective-permute-done.5.refs_4_), channel_id=1, source_target_pairs={{0,1},{1,0},{2,3},{3,2},{4,5},{5,4},{6,7},{7,6},{8,9},{9,8},{10,11... | collective-permute-start | bytes 688136 | tf_op jit(solution)/shard_map/ppermute | solution.py:96
  22.8 9.7 %collective-permute-start.11 = (bf16[32,3584]{1,0:T(8,128)(2,1)S(1)}, bf16[32,3584]{1,0:T(8,128)(2,1)S(1)}, u32[]{:S(2)}, u32[]{:S(2)}) collective-permute-start(bf16[32,3584]{1,0:T(8,128)(2,1)S(1)} %collective-permute-done.5.refs_4_), channel_id=1, source_target_pairs={{0,2},{2,4},{4,6},{6,8},{8,10},{10,12},{12,14},{14,0},{1,15},{3,1}... | collective-permute-start | bytes 688136 | tf_op jit(solution)/shard_map/ppermute | solution.py:99
  25.9 6.7 %collective-permute-start.12 = (bf16[32,3584]{1,0:T(8,128)(2,1)S(1)}, bf16[32,3584]{1,0:T(8,128)(2,1)S(1)}, u32[]{:S(2)}, u32[]{:S(2)}) collective-permute-start(bf16[32,3584]{1,0:T(8,128)(2,1)S(1)} %collective-permute-done.7.refs_5_), channel_id=1, source_target_pairs={{0,1},{1,0},{2,3},{3,2},{4,5},{5,4},{6,7},{7,6},{8,9},{9,8},{10,11... | collective-permute-start | bytes 688136 | tf_op jit(solution)/shard_map/ppermute | solution.py:96
  26.0 6.6 %collective-permute-start.13 = (bf16[32,3584]{1,0:T(8,128)(2,1)S(1)}, bf16[32,3584]{1,0:T(8,128)(2,1)S(1)}, u32[]{:S(2)}, u32[]{:S(2)}) collective-permute-start(bf16[32,3584]{1,0:T(8,128)(2,1)S(1)} %collective-permute-done.7.refs_5_), channel_id=1, source_target_pairs={{0,2},{2,4},{4,6},{6,8},{8,10},{10,12},{12,14},{14,0},{1,15},{3,1}... | collective-permute-start | bytes 688136 | tf_op jit(solution)/shard_map/ppermute | solution.py:99
  28.6 6.6 %collective-permute-start.15 = (bf16[32,3584]{1,0:T(8,128)(2,1)S(1)}, bf16[32,3584]{1,0:T(8,128)(2,1)S(1)}, u32[]{:S(2)}, u32[]{:S(2)}) collective-permute-start(bf16[32,3584]{1,0:T(8,128)(2,1)S(1)} %collective-permute-done.9.refs_6_), channel_id=1, source_target_pairs={{0,2},{2,4},{4,6},{6,8},{8,10},{10,12},{12,14},{14,0},{1,15},{3,1}... | collective-permute-start | bytes 688136 | tf_op jit(solution)/shard_map/ppermute | solution.py:99
  32.6 7.5 %collective-permute-start.18 = (bf16[32,3584]{1,0:T(8,128)(2,1)S(1)}, bf16[32,3584]{1,0:T(8,128)(2,1)S(1)}, u32[]{:S(2)}, u32[]{:S(2)}) collective-permute-start(bf16[32,3584]{1,0:T(8,128)(2,1)S(1)} %collective-permute-done.13.refs_3_), channel_id=1, source_target_pairs={{0,1},{1,0},{2,3},{3,2},{4,5},{5,4},{6,7},{7,6},{8,9},{9,8},{10,11... | collective-permute-start | bytes 688136 | tf_op jit(solution)/shard_map/ppermute | solution.py:96
  35.2 7.6 %collective-permute-start.21 = (bf16[32,3584]{1,0:T(8,128)(2,1)S(1)}, bf16[32,3584]{1,0:T(8,128)(2,1)S(1)}, u32[]{:S(2)}, u32[]{:S(2)}) collective-permute-start(bf16[32,3584]{1,0:T(8,128)(2,1)S(1)} %collective-permute-done.15.refs_4_), channel_id=1, source_target_pairs={{0,1},{1,0},{2,3},{3,2},{4,5},{5,4},{6,7},{7,6},{8,9},{9,8},{10,11... | collective-permute-start | bytes 688136 | tf_op jit(solution)/shard_map/ppermute | solution.py:96
  51.6 18.5 %collective-permute-start.31 = (bf16[96,3584]{1,0:T(8,128)(2,1)S(1)}, bf16[96,3584]{1,0:T(8,128)(2,1)S(1)}, u32[]{:S(2)}, u32[]{:S(2)}) collective-permute-start(bf16[96,3584]{1,0:T(8,128)(2,1)S(1)} %slice.65), channel_id=1, source_target_pairs={{0,1},{1,0},{2,3},{3,2},{4,5},{5,4},{6,7},{7,6},{8,9},{9,8},{10,11... | collective-permute-start | bytes 2064392 | tf_op jit(solution)/shard_map/ppermute | solution.py:96
  59.0 6.2 %collective-permute-start.29 = (bf16[32,3584]{1,0:T(8,128)(2,1)S(1)}, bf16[32,3584]{1,0:T(8,128)(2,1)S(1)}, u32[]{:S(2)}, u32[]{:S(2)}) collective-permute-start(bf16[32,3584]{1,0:T(8,128)(2,1)S(1)} %shard_map.76), channel_id=1, source_target_pairs={{0,2},{2,4},{4,6},{6,8},{8,10},{10,12},{12,14},{14,0},{1,15},{3,1}... | collective-permute-start | bytes 688136 | tf_op jit(solution)/shard_map/ppermute | solution.py:99
  60.2 7.5 %collective-permute-start.30 = (bf16[32,3584]{1,0:T(8,128)(2,1)S(1)}, bf16[32,3584]{1,0:T(8,128)(2,1)S(1)}, u32[]{:S(2)}, u32[]{:S(2)}) collective-permute-start(bf16[32,3584]{1,0:T(8,128)(2,1)S(1)} %shard_map.77), channel_id=1, source_target_pairs={{0,2},{2,4},{4,6},{6,8},{8,10},{10,12},{12,14},{14,0},{1,15},{3,1}... | collective-permute-start | bytes 688136 | tf_op jit(solution)/shard_map/ppermute | solution.py:99
  62.3 7.8 %collective-permute-start.32 = (bf16[32,3584]{1,0:T(8,128)(2,1)S(1)}, bf16[32,3584]{1,0:T(8,128)(2,1)S(1)}, u32[]{:S(2)}, u32[]{:S(2)}) collective-permute-start(bf16[32,3584]{1,0:T(8,128)(2,1)S(1)} %shard_map.78), channel_id=1, source_target_pairs={{0,2},{2,4},{4,6},{6,8},{8,10},{10,12},{12,14},{14,0},{1,15},{3,1}... | collective-permute-start | bytes 688136 | tf_op jit(solution)/shard_map/ppermute | solution.py:99
  65.3 6.8 %collective-permute-start.33 = (bf16[32,3584]{1,0:T(8,128)(2,1)S(1)}, bf16[32,3584]{1,0:T(8,128)(2,1)S(1)}, u32[]{:S(2)}, u32[]{:S(2)}) collective-permute-start(bf16[32,3584]{1,0:T(8,128)(2,1)S(1)} %shard_map.79), channel_id=1, source_target_pairs={{0,2},{2,4},{4,6},{6,8},{8,10},{10,12},{12,14},{14,0},{1,15},{3,1}... | collective-permute-start | bytes 688136 | tf_op jit(solution)/shard_map/ppermute | solution.py:99
  67.8 7.4 %collective-permute-start.34 = (bf16[32,3584]{1,0:T(8,128)(2,1)S(1)}, bf16[32,3584]{1,0:T(8,128)(2,1)S(1)}, u32[]{:S(2)}, u32[]{:S(2)}) collective-permute-start(bf16[32,3584]{1,0:T(8,128)(2,1)S(1)} %shard_map.80), channel_id=1, source_target_pairs={{0,2},{2,4},{4,6},{6,8},{8,10},{10,12},{12,14},{14,0},{1,15},{3,1}... | collective-permute-start | bytes 688136 | tf_op jit(solution)/shard_map/ppermute | solution.py:99
  72.2 5.7 %collective-permute-start.35 = (bf16[32,3584]{1,0:T(8,128)(2,1)S(1)}, bf16[32,3584]{1,0:T(8,128)(2,1)S(1)}, u32[]{:S(2)}, u32[]{:S(2)}) collective-permute-start(bf16[32,3584]{1,0:T(8,128)(2,1)S(1)} %shard_map.81), channel_id=1, source_target_pairs={{0,2},{2,4},{4,6},{6,8},{8,10},{10,12},{12,14},{14,0},{1,15},{3,1}... | collective-permute-start | bytes 688136 | tf_op jit(solution)/shard_map/ppermute | solution.py:99
  75.3 7.4 %collective-permute-start.37 = (bf16[32,3584]{1,0:T(8,128)(2,1)S(1)}, bf16[32,3584]{1,0:T(8,128)(2,1)S(1)}, u32[]{:S(2)}, u32[]{:S(2)}) collective-permute-start(bf16[32,3584]{1,0:T(8,128)(2,1)S(1)} %shard_map.83), channel_id=1, source_target_pairs={{0,2},{2,4},{4,6},{6,8},{8,10},{10,12},{12,14},{14,0},{1,15},{3,1}... | collective-permute-start | bytes 688136 | tf_op jit(solution)/shard_map/ppermute | solution.py:99
  82.7 7.7 %collective-permute-start.38 = (bf16[16,3584]{1,0:T(8,128)(2,1)S(1)}, bf16[16,3584]{1,0:T(8,128)(2,1)S(1)}, u32[]{:S(2)}, u32[]{:S(2)}) collective-permute-start(bf16[16,3584]{1,0:T(8,128)(2,1)S(1)} %shard_map.84), channel_id=1, source_target_pairs={{0,1},{1,0},{2,3},{3,2},{4,5},{5,4},{6,7},{7,6},{8,9},{9,8},{10,11... | collective-permute-start | bytes 344072 | tf_op jit(solution)/shard_map/ppermute | solution.py:96
  (22 other events, 102.8 us)
where the time goes:
time: 91.9 us; the launch traced here: 91.8 us
  starting transfers between devices  57.6 us (63%)
  waiting for transfers between devices  15.4 us (17%)
  matrix products  12.4 us (13%)
  Pallas kernels  2.28 us (2%)
  local copies, waits for them, and re-layouts  1.94 us (2%)
  between operations  1.12 us (1%)
  other arithmetic  1 us (1%)
    ppermute x24, starting transfers between devices, ring(): return lax.ppermute(value, 'tp', ring_pairs)  37.2 us
    ppermute x17, starting transfers between devices, swap(): return lax.ppermute(value, 'tp', swap_pairs)  20.4 us
    ppermute x24, waiting for transfers between devices, ring(): return lax.ppermute(value, 'tp', ring_pairs)  11.6 us
    dot_general x3, matrix products, partial_of(): jnp.dot(hidden, weight, preferred_element_type=f32).astype(bf16)  4.84 us
    dot_general x3, matrix products, hidden_of(): lax.dot_general(rows, weight, (((1,), (1,)), ((), ())), preferred_element...  3.8 us
    ppermute x17, waiting for transfers between devices, swap(): return lax.ppermute(value, 'tp', swap_pairs)  3.79 us
    dot_general x3, matrix products, gate_of(): lax.dot_general(rows, weight, (((1,), (1,)), ((), ())), preferred_element...  3.77 us
    pallas_call x23, Pallas kernels, local(): pl.pallas_call(kernel, out_shape=jax.ShapeDtypeStruct(shape, jnp.bfloat16...  2.28 us
  transfers between devices with their start and end apart: 41, of which 13 were waited for; matrix products, arithmetic and copies ran while one was open for 9% of the time, Pallas kernels for 2%

commit v1 on v0

--- a/solution.py
+++ b/solution.py
@@ -127,8 +127,9 @@
         batch[name] = order(jnp.dot(hidden, weight, preferred_element_type=f32).astype(bf16))
 
     chunks = range(CHUNKS)
+    raw = swap(tokens)
     normed = order(normalize(*order(tokens, norm_gain)))
-    swapped = order(swap(normed))
+    swapped = order(normalize(*order(raw, norm_gain)))
     own, flight = [], []
     for i in chunks:
         rows = slice(i * part, (i + 1) * part)

time: 91.9 us -> 90.7 us (0.987)
  waiting for transfers between devices: 15.4 us -> 14.2 us
    ppermute x17, waiting for transfers between devices: 3.79 us -> 2.54 us  [swap(): return lax.ppermute(value, 'tp', swap_pairs)]
    pallas_call x23 -> x24, Pallas kernels: 2.28 us -> 2.7 us  [local(): pl.pallas_call(kernel, out_shape=jax.ShapeDtypeStruct(shape, jnp.bfloat16...]
  transfers between devices with their start and end apart: 41 -> 41, of which waited for: 13 -> 12; matrix products, arithmetic and copies ran while one was open for 9% -> 9% of each run, Pallas kernels for 2% -> 2%
where the time goes in v1:
time: 90.7 us; the launch traced here: 90.5 us
  starting transfers between devices  57.1 us (63%)
  waiting for transfers between devices  14.2 us (16%)
  matrix products  12.4 us (14%)
  Pallas kernels  2.7 us (3%)
  local copies, waits for them, and re-layouts  1.95 us (2%)
  between operations  1.15 us (1%)
  other arithmetic  1 us (1%)
    ppermute x24, starting transfers between devices, ring(): return lax.ppermute(value, 'tp', ring_pairs)  37.4 us
    ppermute x17, starting transfers between devices, swap(): return lax.ppermute(value, 'tp', swap_pairs)  19.7 us
    ppermute x24, waiting for transfers between devices, ring(): return lax.ppermute(value, 'tp', ring_pairs)  11.6 us
    dot_general x3, matrix products, partial_of(): jnp.dot(hidden, weight, preferred_element_type=f32).astype(bf16)  4.84 us
    dot_general x3, matrix products, hidden_of(): lax.dot_general(rows, weight, (((1,), (1,)), ((), ())), preferred_element...  3.8 us
    dot_general x3, matrix products, gate_of(): lax.dot_general(rows, weight, (((1,), (1,)), ((), ())), preferred_element...  3.79 us
    pallas_call x24, Pallas kernels, local(): pl.pallas_call(kernel, out_shape=jax.ShapeDtypeStruct(shape, jnp.bfloat16...  2.7 us
    ppermute x17, waiting for transfers between devices, swap(): return lax.ppermute(value, 'tp', swap_pairs)  2.54 us
  transfers between devices with their start and end apart: 41, of which 12 were waited for; matrix products, arithmetic and copies ran while one was open for 9% of the time, Pallas kernels for 2%

profile of v1, /device:TPU:1, one launch (start us, length us, event | category | flops | bytes accessed | tf_op | source)
XLA Modules:
  0.0 90.5 jit_solution(15507049274505562177)
XLA Ops:
  0.0 3.2 %collective-permute-start = (bf16[48,3584]{1,0:T(8,128)(2,1)}, bf16[48,3584]{1,0:T(8,128)(2,1)S(1)}, u32[]{:S(2)}, u32[]{:S(2)}) collective-permute-start(bf16[48,3584]{1,0:T(8,128)(2,1)} %tokens_ref), channel_id=1, source_target_pairs={{0,1},{1,0},{2,3},{3,2},{4,5},{5,4},{6,7},{7,6},{8,9},{9,8},{10,11... | collective-permute-start | bytes 1032200 | tf_op jit(solution)/shard_map/ppermute | solution.py:96
  5.9 3.9 %collective-permute-start.1 = (bf16[32,3584]{1,0:T(8,128)(2,1)S(1)}, bf16[32,3584]{1,0:T(8,128)(2,1)S(1)}, u32[]{:S(2)}, u32[]{:S(2)}) collective-permute-start(bf16[32,3584]{1,0:T(8,128)(2,1)S(1)} %shard_map.66.refs_0_), channel_id=1, source_target_pairs={{0,2},{2,4},{4,6},{6,8},{8,10},{10,12},{12,14},{14,0},{1,15},{3,1}... | collective-permute-start | bytes 688136 | tf_op jit(solution)/shard_map/ppermute | solution.py:99
  11.5 1.3 %collective-permute-done.1.refs_3_ = bf16[32,3584]{1,0:T(8,128)(2,1)S(1)} collective-permute-done((bf16[32,3584]{1,0:T(8,128)(2,1)S(1)}, bf16[32,3584]{1,0:T(8,128)(2,1)S(1)}, u32[]{:S(2)}, u32[]{:S(2)}) %collective-permute-start.1) | collective-permute-done | bytes 229408 | tf_op jit(solution)/shard_map/ppermute | solution.py:99
  12.8 1.3 %collective-permute-start.4 = (bf16[32,3584]{1,0:T(8,128)(2,1)S(1)}, bf16[32,3584]{1,0:T(8,128)(2,1)S(1)}, u32[]{:S(2)}, u32[]{:S(2)}) collective-permute-start(bf16[32,3584]{1,0:T(8,128)(2,1)S(1)} %collective-permute-done.1.refs_3_), channel_id=1, source_target_pairs={{0,1},{1,0},{2,3},{3,2},{4,5},{5,4},{6,7},{7,6},{8,9},{9,8},{10,11... | collective-permute-start | bytes 688136 | tf_op jit(solution)/shard_map/ppermute | solution.py:96
  14.1 1.8 %collective-permute-start.5 = (bf16[32,3584]{1,0:T(8,128)(2,1)S(1)}, bf16[32,3584]{1,0:T(8,128)(2,1)S(1)}, u32[]{:S(2)}, u32[]{:S(2)}) collective-permute-start(bf16[32,3584]{1,0:T(8,128)(2,1)S(1)} %collective-permute-done.1.refs_3_), channel_id=1, source_target_pairs={{0,2},{2,4},{4,6},{6,8},{8,10},{10,12},{12,14},{14,0},{1,15},{3,1}... | collective-permute-start | bytes 688136 | tf_op jit(solution)/shard_map/ppermute | solution.py:99
  16.6 1.8 %collective-permute-start.7 = (bf16[32,3584]{1,0:T(8,128)(2,1)S(1)}, bf16[32,3584]{1,0:T(8,128)(2,1)S(1)}, u32[]{:S(2)}, u32[]{:S(2)}) collective-permute-start(bf16[32,3584]{1,0:T(8,128)(2,1)S(1)} %collective-permute-done.2.refs_4_), channel_id=1, source_target_pairs={{0,2},{2,4},{4,6},{6,8},{8,10},{10,12},{12,14},{14,0},{1,15},{3,1}... | collective-permute-start | bytes 688136 | tf_op jit(solution)/shard_map/ppermute | solution.py:99
  19.0 1.8 %collective-permute-start.9 = (bf16[32,3584]{1,0:T(8,128)(2,1)S(1)}, bf16[32,3584]{1,0:T(8,128)(2,1)S(1)}, u32[]{:S(2)}, u32[]{:S(2)}) collective-permute-start(bf16[32,3584]{1,0:T(8,128)(2,1)S(1)} %collective-permute-done.3.refs_5_), channel_id=1, source_target_pairs={{0,2},{2,4},{4,6},{6,8},{8,10},{10,12},{12,14},{14,0},{1,15},{3,1}... | collective-permute-start | bytes 688136 | tf_op jit(solution)/shard_map/ppermute | solution.py:99
  21.5 1.8 %collective-permute-start.11 = (bf16[32,3584]{1,0:T(8,128)(2,1)S(1)}, bf16[32,3584]{1,0:T(8,128)(2,1)S(1)}, u32[]{:S(2)}, u32[]{:S(2)}) collective-permute-start(bf16[32,3584]{1,0:T(8,128)(2,1)S(1)} %collective-permute-done.5.refs_4_), channel_id=1, source_target_pairs={{0,2},{2,4},{4,6},{6,8},{8,10},{10,12},{12,14},{14,0},{1,15},{3,1}... | collective-permute-start | bytes 688136 | tf_op jit(solution)/shard_map/ppermute | solution.py:99
  27.4 2.3 %collective-permute-start.15 = (bf16[32,3584]{1,0:T(8,128)(2,1)S(1)}, bf16[32,3584]{1,0:T(8,128)(2,1)S(1)}, u32[]{:S(2)}, u32[]{:S(2)}) collective-permute-start(bf16[32,3584]{1,0:T(8,128)(2,1)S(1)} %collective-permute-done.9.refs_6_), channel_id=1, source_target_pairs={{0,2},{2,4},{4,6},{6,8},{8,10},{10,12},{12,14},{14,0},{1,15},{3,1}... | collective-permute-start | bytes 688136 | tf_op jit(solution)/shard_map/ppermute | solution.py:99
  29.7 1.6 %convolution_convert_fusion.2.refs_0_ = bf16[256,3584]{1,0:T(8,128)(2,1)S(1)} fusion(bf16[256,576]{0,1:T(8,128)(2,1)S(1)} %fusion, bf16[576,3584]{1,0:T(8,128)(2,1)S(1)} %copy-done.2), kind=kOutput, calls=%fused_computation.2 | convolution fusion | flops 1057882112 | bytes 6258688 | tf_op jit(solution)/shard_map/dot_general | solution.py:127
  38.8 1.6 %convolution_convert_fusion.1.refs_0_ = bf16[256,3584]{1,0:T(8,128)(2,1)S(1)} fusion(bf16[256,576]{0,1:T(8,128)(2,1)S(1)} %fusion.1, bf16[576,3584]{1,0:T(8,128)(2,1)S(1)} %copy-done.2), kind=kOutput, calls=%fused_computation.1 | convolution fusion | flops 1057882112 | bytes 6258688 | tf_op jit(solution)/shard_map/dot_general | solution.py:127
  41.6 2.2 %collective-permute-start.22 = (bf16[48,3584]{1,0:T(8,128)(2,1)S(1)}, bf16[48,3584]{1,0:T(8,128)(2,1)S(1)}, u32[]{:S(2)}, u32[]{:S(2)}) collective-permute-start(bf16[48,3584]{1,0:T(8,128)(2,1)S(1)} %shard_map.71.refs_5_), channel_id=1, source_target_pairs={{0,1},{1,0},{2,3},{3,2},{4,5},{5,4},{6,7},{7,6},{8,9},{9,8},{10,11... | collective-permute-start | bytes 1032200 | tf_op jit(solution)/shard_map/ppermute | solution.py:96
  43.9 1.3 %collective-permute-done.22.refs_6_ = bf16[48,3584]{1,0:T(8,128)(2,1)S(1)} collective-permute-done((bf16[48,3584]{1,0:T(8,128)(2,1)S(1)}, bf16[48,3584]{1,0:T(8,128)(2,1)S(1)}, u32[]{:S(2)}, u32[]{:S(2)}) %collective-permute-start.22) | collective-permute-done | bytes 344096 | tf_op jit(solution)/shard_map/ppermute | solution.py:96
  47.9 1.6 %convolution_convert_fusion.refs_0_ = bf16[256,3584]{1,0:T(8,128)(2,1)S(1)} fusion(bf16[256,576]{0,1:T(8,128)(2,1)S(1)} %fusion.2, bf16[576,3584]{1,0:T(8,128)(2,1)S(1)} %copy-done.2), kind=kOutput, calls=%fused_computation | convolution fusion | flops 1057882112 | bytes 6258688 | tf_op jit(solution)/shard_map/dot_general | solution.py:127
  55.8 1.8 %collective-permute-start.28 = (bf16[32,3584]{1,0:T(8,128)(2,1)S(1)}, bf16[32,3584]{1,0:T(8,128)(2,1)S(1)}, u32[]{:S(2)}, u32[]{:S(2)}) collective-permute-start(bf16[32,3584]{1,0:T(8,128)(2,1)S(1)} %shard_map.76), channel_id=1, source_target_pairs={{0,2},{2,4},{4,6},{6,8},{8,10},{10,12},{12,14},{14,0},{1,15},{3,1}... | collective-permute-start | bytes 688136 | tf_op jit(solution)/shard_map/ppermute | solution.py:99
  61.0 2.9 %collective-permute-start.32 = (bf16[32,3584]{1,0:T(8,128)(2,1)S(1)}, bf16[32,3584]{1,0:T(8,128)(2,1)S(1)}, u32[]{:S(2)}, u32[]{:S(2)}) collective-permute-start(bf16[32,3584]{1,0:T(8,128)(2,1)S(1)} %shard_map.79), channel_id=1, source_target_pairs={{0,2},{2,4},{4,6},{6,8},{8,10},{10,12},{12,14},{14,0},{1,15},{3,1}... | collective-permute-start | bytes 688136 | tf_op jit(solution)/shard_map/ppermute | solution.py:99
  64.1 2.3 %collective-permute-start.33 = (bf16[32,3584]{1,0:T(8,128)(2,1)S(1)}, bf16[32,3584]{1,0:T(8,128)(2,1)S(1)}, u32[]{:S(2)}, u32[]{:S(2)}) collective-permute-start(bf16[32,3584]{1,0:T(8,128)(2,1)S(1)} %shard_map.80), channel_id=1, source_target_pairs={{0,2},{2,4},{4,6},{6,8},{8,10},{10,12},{12,14},{14,0},{1,15},{3,1}... | collective-permute-start | bytes 688136 | tf_op jit(solution)/shard_map/ppermute | solution.py:99
  66.5 2.3 %collective-permute-start.34 = (bf16[32,3584]{1,0:T(8,128)(2,1)S(1)}, bf16[32,3584]{1,0:T(8,128)(2,1)S(1)}, u32[]{:S(2)}, u32[]{:S(2)}) collective-permute-start(bf16[32,3584]{1,0:T(8,128)(2,1)S(1)} %shard_map.81), channel_id=1, source_target_pairs={{0,2},{2,4},{4,6},{6,8},{8,10},{10,12},{12,14},{14,0},{1,15},{3,1}... | collective-permute-start | bytes 688136 | tf_op jit(solution)/shard_map/ppermute | solution.py:99
  69.0 1.9 %collective-permute-done.33.refs_2_ = bf16[32,3584]{1,0:T(8,128)(2,1)S(1)} collective-permute-done((bf16[32,3584]{1,0:T(8,128)(2,1)S(1)}, bf16[32,3584]{1,0:T(8,128)(2,1)S(1)}, u32[]{:S(2)}, u32[]{:S(2)}) %collective-permute-start.33) | collective-permute-done | bytes 229408 | tf_op jit(solution)/shard_map/ppermute | solution.py:99
  70.9 2.7 %collective-permute-start.35 = (bf16[32,3584]{1,0:T(8,128)(2,1)S(1)}, bf16[32,3584]{1,0:T(8,128)(2,1)S(1)}, u32[]{:S(2)}, u32[]{:S(2)}) collective-permute-start(bf16[32,3584]{1,0:T(8,128)(2,1)S(1)} %shard_map.82), channel_id=1, source_target_pairs={{0,2},{2,4},{4,6},{6,8},{8,10},{10,12},{12,14},{14,0},{1,15},{3,1}... | collective-permute-start | bytes 688136 | tf_op jit(solution)/shard_map/ppermute | solution.py:99
  74.0 2.2 %collective-permute-start.37 = (bf16[32,3584]{1,0:T(8,128)(2,1)S(1)}, bf16[32,3584]{1,0:T(8,128)(2,1)S(1)}, u32[]{:S(2)}, u32[]{:S(2)}) collective-permute-start(bf16[32,3584]{1,0:T(8,128)(2,1)S(1)} %shard_map.84), channel_id=1, source_target_pairs={{0,2},{2,4},{4,6},{6,8},{8,10},{10,12},{12,14},{14,0},{1,15},{3,1}... | collective-permute-start | bytes 688136 | tf_op jit(solution)/shard_map/ppermute | solution.py:99
  76.6 2.4 %collective-permute-done.36.refs_1_ = bf16[32,3584]{1,0:T(8,128)(2,1)S(1)} collective-permute-done((bf16[32,3584]{1,0:T(8,128)(2,1)S(1)}, bf16[32,3584]{1,0:T(8,128)(2,1)S(1)}, u32[]{:S(2)}, u32[]{:S(2)}) %collective-permute-start.36) | collective-permute-done | bytes 229408 | tf_op jit(solution)/shard_map/ppermute | solution.py:99
  79.1 2.4 %collective-permute-done.37.refs_1_ = bf16[32,3584]{1,0:T(8,128)(2,1)S(1)} collective-permute-done((bf16[32,3584]{1,0:T(8,128)(2,1)S(1)}, bf16[32,3584]{1,0:T(8,128)(2,1)S(1)}, u32[]{:S(2)}, u32[]{:S(2)}) %collective-permute-start.37) | collective-permute-done | bytes 229408 | tf_op jit(solution)/shard_map/ppermute | solution.py:99
  81.5 6.4 %collective-permute-start.38 = (bf16[16,3584]{1,0:T(8,128)(2,1)S(1)}, bf16[16,3584]{1,0:T(8,128)(2,1)S(1)}, u32[]{:S(2)}, u32[]{:S(2)}) collective-permute-start(bf16[16,3584]{1,0:T(8,128)(2,1)S(1)} %shard_map.85), channel_id=1, source_target_pairs={{0,1},{1,0},{2,3},{3,2},{4,5},{5,4},{6,7},{7,6},{8,9},{9,8},{10,11... | collective-permute-start | bytes 344072 | tf_op jit(solution)/shard_map/ppermute | solution.py:96
  (113 shorter events, 34.3 us)
Async XLA Ops:
  5.9 6.9 %collective-permute-start.1 = (bf16[32,3584]{1,0:T(8,128)(2,1)S(1)}, bf16[32,3584]{1,0:T(8,128)(2,1)S(1)}, u32[]{:S(2)}, u32[]{:S(2)}) collective-permute-start(bf16[32,3584]{1,0:T(8,128)(2,1)S(1)} %shard_map.66.refs_0_), channel_id=1, source_target_pairs={{0,2},{2,4},{4,6},{6,8},{8,10},{10,12},{12,14},{14,0},{1,15},{3,1}... | collective-permute-start | bytes 688136 | tf_op jit(solution)/shard_map/ppermute | solution.py:99
  9.9 6.1 %collective-permute-start.2 = (bf16[32,3584]{1,0:T(8,128)(2,1)S(1)}, bf16[32,3584]{1,0:T(8,128)(2,1)S(1)}, u32[]{:S(2)}, u32[]{:S(2)}) collective-permute-start(bf16[32,3584]{1,0:T(8,128)(2,1)S(1)} %shard_map.67.refs_1_), channel_id=1, source_target_pairs={{0,2},{2,4},{4,6},{6,8},{8,10},{10,12},{12,14},{14,0},{1,15},{3,1}... | collective-permute-start | bytes 688136 | tf_op jit(solution)/shard_map/ppermute | solution.py:99
  10.7 7.7 %collective-permute-start.3 = (bf16[32,3584]{1,0:T(8,128)(2,1)S(1)}, bf16[32,3584]{1,0:T(8,128)(2,1)S(1)}, u32[]{:S(2)}, u32[]{:S(2)}) collective-permute-start(bf16[32,3584]{1,0:T(8,128)(2,1)S(1)} %shard_map.68.refs_2_), channel_id=1, source_target_pairs={{0,2},{2,4},{4,6},{6,8},{8,10},{10,12},{12,14},{14,0},{1,15},{3,1}... | collective-permute-start | bytes 688136 | tf_op jit(solution)/shard_map/ppermute | solution.py:99
  12.8 6.2 %collective-permute-start.4 = (bf16[32,3584]{1,0:T(8,128)(2,1)S(1)}, bf16[32,3584]{1,0:T(8,128)(2,1)S(1)}, u32[]{:S(2)}, u32[]{:S(2)}) collective-permute-start(bf16[32,3584]{1,0:T(8,128)(2,1)S(1)} %collective-permute-done.1.refs_3_), channel_id=1, source_target_pairs={{0,1},{1,0},{2,3},{3,2},{4,5},{5,4},{6,7},{7,6},{8,9},{9,8},{10,11... | collective-permute-start | bytes 688136 | tf_op jit(solution)/shard_map/ppermute | solution.py:96
  14.1 6.7 %collective-permute-start.5 = (bf16[32,3584]{1,0:T(8,128)(2,1)S(1)}, bf16[32,3584]{1,0:T(8,128)(2,1)S(1)}, u32[]{:S(2)}, u32[]{:S(2)}) collective-permute-start(bf16[32,3584]{1,0:T(8,128)(2,1)S(1)} %collective-permute-done.1.refs_3_), channel_id=1, source_target_pairs={{0,2},{2,4},{4,6},{6,8},{8,10},{10,12},{12,14},{14,0},{1,15},{3,1}... | collective-permute-start | bytes 688136 | tf_op jit(solution)/shard_map/ppermute | solution.py:99
  16.6 8.2 %collective-permute-start.7 = (bf16[32,3584]{1,0:T(8,128)(2,1)S(1)}, bf16[32,3584]{1,0:T(8,128)(2,1)S(1)}, u32[]{:S(2)}, u32[]{:S(2)}) collective-permute-start(bf16[32,3584]{1,0:T(8,128)(2,1)S(1)} %collective-permute-done.2.refs_4_), channel_id=1, source_target_pairs={{0,2},{2,4},{4,6},{6,8},{8,10},{10,12},{12,14},{14,0},{1,15},{3,1}... | collective-permute-start | bytes 688136 | tf_op jit(solution)/shard_map/ppermute | solution.py:99
  18.4 6.5 %collective-permute-start.8 = (bf16[32,3584]{1,0:T(8,128)(2,1)S(1)}, bf16[32,3584]{1,0:T(8,128)(2,1)S(1)}, u32[]{:S(2)}, u32[]{:S(2)}) collective-permute-start(bf16[32,3584]{1,0:T(8,128)(2,1)S(1)} %collective-permute-done.3.refs_5_), channel_id=1, source_target_pairs={{0,1},{1,0},{2,3},{3,2},{4,5},{5,4},{6,7},{7,6},{8,9},{9,8},{10,11... | collective-permute-start | bytes 688136 | tf_op jit(solution)/shard_map/ppermute | solution.py:96
  19.0 8.2 %collective-permute-start.9 = (bf16[32,3584]{1,0:T(8,128)(2,1)S(1)}, bf16[32,3584]{1,0:T(8,128)(2,1)S(1)}, u32[]{:S(2)}, u32[]{:S(2)}) collective-permute-start(bf16[32,3584]{1,0:T(8,128)(2,1)S(1)} %collective-permute-done.3.refs_5_), channel_id=1, source_target_pairs={{0,2},{2,4},{4,6},{6,8},{8,10},{10,12},{12,14},{14,0},{1,15},{3,1}... | collective-permute-start | bytes 688136 | tf_op jit(solution)/shard_map/ppermute | solution.py:99
  20.8 6.5 %collective-permute-start.10 = (bf16[32,3584]{1,0:T(8,128)(2,1)S(1)}, bf16[32,3584]{1,0:T(8,128)(2,1)S(1)}, u32[]{:S(2)}, u32[]{:S(2)}) collective-permute-start(bf16[32,3584]{1,0:T(8,128)(2,1)S(1)} %collective-permute-done.5.refs_4_), channel_id=1, source_target_pairs={{0,1},{1,0},{2,3},{3,2},{4,5},{5,4},{6,7},{7,6},{8,9},{9,8},{10,11... | collective-permute-start | bytes 688136 | tf_op jit(solution)/shard_map/ppermute | solution.py:96
  21.5 9.8 %collective-permute-start.11 = (bf16[32,3584]{1,0:T(8,128)(2,1)S(1)}, bf16[32,3584]{1,0:T(8,128)(2,1)S(1)}, u32[]{:S(2)}, u32[]{:S(2)}) collective-permute-start(bf16[32,3584]{1,0:T(8,128)(2,1)S(1)} %collective-permute-done.5.refs_4_), channel_id=1, source_target_pairs={{0,2},{2,4},{4,6},{6,8},{8,10},{10,12},{12,14},{14,0},{1,15},{3,1}... | collective-permute-start | bytes 688136 | tf_op jit(solution)/shard_map/ppermute | solution.py:99
  24.7 6.7 %collective-permute-start.12 = (bf16[32,3584]{1,0:T(8,128)(2,1)S(1)}, bf16[32,3584]{1,0:T(8,128)(2,1)S(1)}, u32[]{:S(2)}, u32[]{:S(2)}) collective-permute-start(bf16[32,3584]{1,0:T(8,128)(2,1)S(1)} %collective-permute-done.7.refs_5_), channel_id=1, source_target_pairs={{0,1},{1,0},{2,3},{3,2},{4,5},{5,4},{6,7},{7,6},{8,9},{9,8},{10,11... | collective-permute-start | bytes 688136 | tf_op jit(solution)/shard_map/ppermute | solution.py:96
  24.9 6.6 %collective-permute-start.13 = (bf16[32,3584]{1,0:T(8,128)(2,1)S(1)}, bf16[32,3584]{1,0:T(8,128)(2,1)S(1)}, u32[]{:S(2)}, u32[]{:S(2)}) collective-permute-start(bf16[32,3584]{1,0:T(8,128)(2,1)S(1)} %collective-permute-done.7.refs_5_), channel_id=1, source_target_pairs={{0,2},{2,4},{4,6},{6,8},{8,10},{10,12},{12,14},{14,0},{1,15},{3,1}... | collective-permute-start | bytes 688136 | tf_op jit(solution)/shard_map/ppermute | solution.py:99
  27.4 6.6 %collective-permute-start.15 = (bf16[32,3584]{1,0:T(8,128)(2,1)S(1)}, bf16[32,3584]{1,0:T(8,128)(2,1)S(1)}, u32[]{:S(2)}, u32[]{:S(2)}) collective-permute-start(bf16[32,3584]{1,0:T(8,128)(2,1)S(1)} %collective-permute-done.9.refs_6_), channel_id=1, source_target_pairs={{0,2},{2,4},{4,6},{6,8},{8,10},{10,12},{12,14},{14,0},{1,15},{3,1}... | collective-permute-start | bytes 688136 | tf_op jit(solution)/shard_map/ppermute | solution.py:99
  31.4 7.4 %collective-permute-start.18 = (bf16[32,3584]{1,0:T(8,128)(2,1)S(1)}, bf16[32,3584]{1,0:T(8,128)(2,1)S(1)}, u32[]{:S(2)}, u32[]{:S(2)}) collective-permute-start(bf16[32,3584]{1,0:T(8,128)(2,1)S(1)} %collective-permute-done.13.refs_3_), channel_id=1, source_target_pairs={{0,1},{1,0},{2,3},{3,2},{4,5},{5,4},{6,7},{7,6},{8,9},{9,8},{10,11... | collective-permute-start | bytes 688136 | tf_op jit(solution)/shard_map/ppermute | solution.py:96
  34.0 7.6 %collective-permute-start.21 = (bf16[32,3584]{1,0:T(8,128)(2,1)S(1)}, bf16[32,3584]{1,0:T(8,128)(2,1)S(1)}, u32[]{:S(2)}, u32[]{:S(2)}) collective-permute-start(bf16[32,3584]{1,0:T(8,128)(2,1)S(1)} %collective-permute-done.15.refs_4_), channel_id=1, source_target_pairs={{0,1},{1,0},{2,3},{3,2},{4,5},{5,4},{6,7},{7,6},{8,9},{9,8},{10,11... | collective-permute-start | bytes 688136 | tf_op jit(solution)/shard_map/ppermute | solution.py:96
  50.3 18.5 %collective-permute-start.31 = (bf16[96,3584]{1,0:T(8,128)(2,1)S(1)}, bf16[96,3584]{1,0:T(8,128)(2,1)S(1)}, u32[]{:S(2)}, u32[]{:S(2)}) collective-permute-start(bf16[96,3584]{1,0:T(8,128)(2,1)S(1)} %slice.65), channel_id=1, source_target_pairs={{0,1},{1,0},{2,3},{3,2},{4,5},{5,4},{6,7},{7,6},{8,9},{9,8},{10,11... | collective-permute-start | bytes 2064392 | tf_op jit(solution)/shard_map/ppermute | solution.py:96
  57.8 6.2 %collective-permute-start.29 = (bf16[32,3584]{1,0:T(8,128)(2,1)S(1)}, bf16[32,3584]{1,0:T(8,128)(2,1)S(1)}, u32[]{:S(2)}, u32[]{:S(2)}) collective-permute-start(bf16[32,3584]{1,0:T(8,128)(2,1)S(1)} %shard_map.77), channel_id=1, source_target_pairs={{0,2},{2,4},{4,6},{6,8},{8,10},{10,12},{12,14},{14,0},{1,15},{3,1}... | collective-permute-start | bytes 688136 | tf_op jit(solution)/shard_map/ppermute | solution.py:99
  59.0 7.5 %collective-permute-start.30 = (bf16[32,3584]{1,0:T(8,128)(2,1)S(1)}, bf16[32,3584]{1,0:T(8,128)(2,1)S(1)}, u32[]{:S(2)}, u32[]{:S(2)}) collective-permute-start(bf16[32,3584]{1,0:T(8,128)(2,1)S(1)} %shard_map.78), channel_id=1, source_target_pairs={{0,2},{2,4},{4,6},{6,8},{8,10},{10,12},{12,14},{14,0},{1,15},{3,1}... | collective-permute-start | bytes 688136 | tf_op jit(solution)/shard_map/ppermute | solution.py:99
  61.0 7.8 %collective-permute-start.32 = (bf16[32,3584]{1,0:T(8,128)(2,1)S(1)}, bf16[32,3584]{1,0:T(8,128)(2,1)S(1)}, u32[]{:S(2)}, u32[]{:S(2)}) collective-permute-start(bf16[32,3584]{1,0:T(8,128)(2,1)S(1)} %shard_map.79), channel_id=1, source_target_pairs={{0,2},{2,4},{4,6},{6,8},{8,10},{10,12},{12,14},{14,0},{1,15},{3,1}... | collective-permute-start | bytes 688136 | tf_op jit(solution)/shard_map/ppermute | solution.py:99
  64.1 6.8 %collective-permute-start.33 = (bf16[32,3584]{1,0:T(8,128)(2,1)S(1)}, bf16[32,3584]{1,0:T(8,128)(2,1)S(1)}, u32[]{:S(2)}, u32[]{:S(2)}) collective-permute-start(bf16[32,3584]{1,0:T(8,128)(2,1)S(1)} %shard_map.80), channel_id=1, source_target_pairs={{0,2},{2,4},{4,6},{6,8},{8,10},{10,12},{12,14},{14,0},{1,15},{3,1}... | collective-permute-start | bytes 688136 | tf_op jit(solution)/shard_map/ppermute | solution.py:99
  66.5 7.4 %collective-permute-start.34 = (bf16[32,3584]{1,0:T(8,128)(2,1)S(1)}, bf16[32,3584]{1,0:T(8,128)(2,1)S(1)}, u32[]{:S(2)}, u32[]{:S(2)}) collective-permute-start(bf16[32,3584]{1,0:T(8,128)(2,1)S(1)} %shard_map.81), channel_id=1, source_target_pairs={{0,2},{2,4},{4,6},{6,8},{8,10},{10,12},{12,14},{14,0},{1,15},{3,1}... | collective-permute-start | bytes 688136 | tf_op jit(solution)/shard_map/ppermute | solution.py:99
  70.9 5.7 %collective-permute-start.35 = (bf16[32,3584]{1,0:T(8,128)(2,1)S(1)}, bf16[32,3584]{1,0:T(8,128)(2,1)S(1)}, u32[]{:S(2)}, u32[]{:S(2)}) collective-permute-start(bf16[32,3584]{1,0:T(8,128)(2,1)S(1)} %shard_map.82), channel_id=1, source_target_pairs={{0,2},{2,4},{4,6},{6,8},{8,10},{10,12},{12,14},{14,0},{1,15},{3,1}... | collective-permute-start | bytes 688136 | tf_op jit(solution)/shard_map/ppermute | solution.py:99
  74.0 7.4 %collective-permute-start.37 = (bf16[32,3584]{1,0:T(8,128)(2,1)S(1)}, bf16[32,3584]{1,0:T(8,128)(2,1)S(1)}, u32[]{:S(2)}, u32[]{:S(2)}) collective-permute-start(bf16[32,3584]{1,0:T(8,128)(2,1)S(1)} %shard_map.84), channel_id=1, source_target_pairs={{0,2},{2,4},{4,6},{6,8},{8,10},{10,12},{12,14},{14,0},{1,15},{3,1}... | collective-permute-start | bytes 688136 | tf_op jit(solution)/shard_map/ppermute | solution.py:99
  81.5 7.7 %collective-permute-start.38 = (bf16[16,3584]{1,0:T(8,128)(2,1)S(1)}, bf16[16,3584]{1,0:T(8,128)(2,1)S(1)}, u32[]{:S(2)}, u32[]{:S(2)}) collective-permute-start(bf16[16,3584]{1,0:T(8,128)(2,1)S(1)} %shard_map.85), channel_id=1, source_target_pairs={{0,1},{1,0},{2,3},{3,2},{4,5},{5,4},{6,7},{7,6},{8,9},{9,8},{10,11... | collective-permute-start | bytes 344072 | tf_op jit(solution)/shard_map/ppermute | solution.py:96
  (22 other events, 98.6 us)
